TPU v7x, 32 devices: a whole 2x2x4 slice. The times are simulated.
32 devices in a mesh: groups: 2 (over x), gx: 4 (over y, core), gy: 4 (over z).
Axes of the slice: x: 2, y: 2, z: 4, core: 2. Of those that a mesh axis runs over, the one named last changes fastest.
Arguments:
- inputs: bfloat16 [32, 16, 58, 128], P(('groups', 'gx'), 'gy'), parts along dimension 0, may hold values from -6 to 6
- target: bfloat16 [32, 16, 53, 128], P(('groups', 'gx'), 'gy'), parts along dimension 0, may hold values from -6 to 6
- w_first: bfloat16 [3, 3, 3, 58, 64], replicated, may hold values from -0.15625 to 0.15625
- w_second: bfloat16 [3, 3, 3, 64, 53], replicated, may hold values from -0.15625 to 0.15625
Outputs:
- prediction: bfloat16 [32, 16, 53, 128], P(('groups', 'gx'), 'gy'), parts along dimension 0
- grad_first: float32 [6, 3, 3, 58, 64], P('groups'), parts along dimension 0
- grad_second: float32 [6, 3, 3, 64, 53], P('groups'), parts along dimension 0
There are 2 independent parts, one for each index of `groups`. A program takes and returns all parts, laid end to end along the dimension named above; an argument that names none is the same for every part. Nothing has to cross between parts.
All inputs are finite; a program needn't handle non-finite values.
Results may differ from a plain program's by a relative error of at most 0.0049.
Values may be sent and summed in bfloat16 or wider, within the bound.
A program may use at most 64 MiB of HBM per device.

v0:
```python
import math

import jax
import jax.numpy as jnp
from jax import lax
from jax.sharding import PartitionSpec as P

root_two_pi = 0.7978845608028654
cubic_term = 0.044715


def extended(cells, sides, width):
    for axis, dim in sides:
        count = lax.axis_size(axis)
        ends = count - 1
        head = lax.slice_in_dim(cells, 0, width, axis=dim)
        tail = lax.slice_in_dim(cells, cells.shape[dim] - width, cells.shape[dim], axis=dim)
        cells = jnp.concatenate(
            [
                lax.ppermute(tail, axis, [(i, (i + 1) % count) for i in range(ends)]),
                cells,
                lax.ppermute(head, axis, [((i + 1) % count, i) for i in range(ends)]),
            ],
            axis=dim,
        )
    return cells


def shifted(value, axis, steps):
    count = lax.axis_size(axis)
    leading, last = (max(0, -steps), min(count, count - steps))
    return lax.ppermute(value, axis, [(source, source + steps) for source in range(leading, last)])


def smooth_gate(activation):
    tangent = jnp.tanh(
        root_two_pi * (activation + cubic_term * activation * activation * activation)
    )
    return 0.5 * activation * (1.0 + tangent)


def gate_slope(activation):
    tangent = jnp.tanh(
        root_two_pi * (activation + cubic_term * activation * activation * activation)
    )
    return 0.5 * (1.0 + tangent) + 0.5 * activation * (1.0 - tangent * tangent) * root_two_pi * (
        1.0 + 3.0 * cubic_term * activation * activation
    )


def depth_padded(field):
    return jnp.pad(field, ((0, 0), (0, 0), (0, 0), (1, 1)))


def correlate(field, kernel):
    extent_x = field.shape[0] - 2
    extent_y = field.shape[1] - 2
    depth = field.shape[3]
    padded = depth_padded(field)
    total = jnp.zeros((extent_x, extent_y, kernel.shape[4], depth), jnp.float32)
    for step_a in range(3):
        for step_b in range(3):
            for step_c in range(3):
                window = padded[
                    step_a : step_a + extent_x,
                    step_b : step_b + extent_y,
                    :,
                    step_c : step_c + depth,
                ]
                total = total + jnp.einsum(
                    "xycz,co->xyoz",
                    window,
                    kernel[step_a, step_b, step_c],
                    preferred_element_type=jnp.float32,
                )
    return total


def correlate_back(field, kernel):
    extent_x = field.shape[0] - 2
    extent_y = field.shape[1] - 2
    depth = field.shape[3]
    padded = depth_padded(field)
    total = jnp.zeros((extent_x, extent_y, kernel.shape[3], depth), jnp.float32)
    for step_a in range(3):
        for step_b in range(3):
            for step_c in range(3):
                window = padded[
                    2 - step_a : 2 - step_a + extent_x,
                    2 - step_b : 2 - step_b + extent_y,
                    :,
                    2 - step_c : 2 - step_c + depth,
                ]
                total = total + jnp.einsum(
                    "xyoz,io->xyiz",
                    window,
                    kernel[step_a, step_b, step_c],
                    preferred_element_type=jnp.float32,
                )
    return total


def filter_grad(field, slope_term):
    extent_x = slope_term.shape[0]
    extent_y = slope_term.shape[1]
    depth = slope_term.shape[3]
    padded = depth_padded(field)
    planes = []
    for step_a in range(3):
        rows_b = []
        for step_b in range(3):
            rows_c = []
            for step_c in range(3):
                window = padded[
                    step_a : step_a + extent_x,
                    step_b : step_b + extent_y,
                    :,
                    step_c : step_c + depth,
                ]
                rows_c.append(
                    jnp.einsum(
                        "xycz,xyoz->co", window, slope_term, preferred_element_type=jnp.float32
                    )
                )
            rows_b.append(jnp.stack(rows_c))
        planes.append(jnp.stack(rows_b))
    return jnp.stack(planes)


def on_device(inputs, target, w_first, w_second):
    block_x = inputs.shape[0]
    block_y = inputs.shape[1]
    padded_in = extended(inputs, (("gx", 0), ("gy", 1)), 1)
    activation = correlate(padded_in, w_first)
    hidden = smooth_gate(activation).astype(jnp.bfloat16)
    padded_hidden = extended(hidden, (("gx", 0), ("gy", 1)), 1)
    output = correlate(padded_hidden, w_second)
    prediction = output.astype(jnp.bfloat16)
    cell_count = block_x * lax.axis_size("gx") * block_y * lax.axis_size("gy") * inputs.shape[3]
    normalizer = 1.0 / math.sqrt(cell_count)
    output_grad = ((output - target.astype(jnp.float32)) * normalizer).astype(jnp.bfloat16)
    grad_second = filter_grad(padded_hidden, output_grad)
    widened = jnp.pad(output_grad, ((2, 2), (2, 2), (0, 0), (0, 0)))
    spread = correlate_back(widened, w_second)
    extent_x = spread.shape[0]
    from_below = shifted(spread[extent_x - 1 :].astype(jnp.bfloat16), "gx", 1).astype(jnp.float32)
    from_above = shifted(spread[:1].astype(jnp.bfloat16), "gx", -1).astype(jnp.float32)
    summed_x = spread[1 : extent_x - 1]
    summed_x = summed_x.at[:1].add(from_below).at[-1:].add(from_above)
    extent_y = summed_x.shape[1]
    from_left = shifted(summed_x[:, extent_y - 1 :].astype(jnp.bfloat16), "gy", 1).astype(
        jnp.float32
    )
    from_right = shifted(summed_x[:, :1].astype(jnp.bfloat16), "gy", -1).astype(jnp.float32)
    back_grad = summed_x[:, 1 : extent_y - 1].at[:, :1].add(from_left).at[:, -1:].add(from_right)
    slope_term = (back_grad * gate_slope(activation)).astype(jnp.bfloat16)
    grad_first = filter_grad(padded_in, slope_term)
    grad_first, grad_second = lax.psum((grad_first, grad_second), ("gx", "gy"))
    return (prediction, grad_first, grad_second)


def solution(mesh):
    placed = (
        P(("groups", "gx"), "gy", None, None),
        P(("groups", "gx"), "gy", None, None),
        P(),
        P(),
    )
    return jax.shard_map(
        on_device,
        mesh=mesh,
        in_specs=placed,
        out_specs=(
            P(("groups", "gx"), "gy", None, None),
            P("groups", None, None, None, None),
            P("groups", None, None, None, None),
        ),
        check_vma=False,
    )
```

profile of v0, /device:TPU:1, one launch (start us, length us, event | category | flops | bytes accessed | tf_op | source)
XLA Modules:
  0.0 206.0 jit_solution(16586595825704326842)
XLA Ops:
  7.2 0.9 fusion.357
  8.2 4.5 %collective-permute-start = (bf16[1,4,58,128]{3,2,1,0:T(8,128)(2,1)S(1)}, bf16[1,4,58,128]{3,2,1,0:T(8,128)(2,1)S(1)}, u32[]{:S(2)}, u32[]{:S(2)}) collective-permute-start(bf16[1,4,58,128]{3,2,1,0:T(8,128)(2,1)S(1)} %copy.188), channel_id=1, source_target_pairs={{0,4},{4,8},{8,12},{1,5},{5,9},{9,13},{2,6},{6,10},{10,14},{3,7},{... | collective-permute-start | bytes 178184 | tf_op jit(solution)/shard_map/ppermute | solution.py:20
  12.7 1.9 collective-permute-start.1
  14.7 1.2 constant_dynamic-update-slice_fusion.6
  15.9 2.4 %collective-permute-done.1 = bf16[1,4,58,128]{3,2,1,0:T(8,128)(2,1)S(1)} collective-permute-done((bf16[1,4,58,128]{3,2,1,0:T(8,128)(2,1)S(1)}, bf16[1,4,58,128]{3,2,1,0:T(8,128)(2,1)S(1)}, u32[]{:S(2)}, u32[]{:S(2)}) %collective-permute-start.1) | collective-permute-done | bytes 59424 | tf_op jit(solution)/shard_map/ppermute | solution.py:22
  18.4 3.2 %collective-permute-start.2 = (bf16[6,1,58,128]{3,2,1,0:T(8,128)(2,1)S(1)}, bf16[6,1,58,128]{3,2,1,0:T(8,128)(2,1)S(1)}, u32[]{:S(2)}, u32[]{:S(2)}) collective-permute-start(bf16[6,1,58,128]{3,2,1,0:T(8,128)(2,1)S(1)} %get-tuple-element.64), channel_id=1, source_target_pairs={{0,1},{1,2},{2,3},{4,5},{5,6},{6,7},{8,9},{9,10},{10,11},{12,13},{... | collective-permute-start | bytes 267272 | tf_op jit(solution)/shard_map/ppermute | solution.py:20
  21.6 1.3 collective-permute-start.3
  23.2 3.7 %collective-permute-done.3 = bf16[6,1,58,128]{3,2,1,0:T(8,128)(2,1)S(1)} collective-permute-done((bf16[6,1,58,128]{3,2,1,0:T(8,128)(2,1)S(1)}, bf16[6,1,58,128]{3,2,1,0:T(8,128)(2,1)S(1)}, u32[]{:S(2)}, u32[]{:S(2)}) %collective-permute-start.3) | collective-permute-done | bytes 89120 | tf_op jit(solution)/shard_map/ppermute | solution.py:22
  27.0 0.6 fusion.57
  29.1 0.3 convolution_bitcast_fusion.17
  30.1 0.3 convolution_bitcast_fusion.15
  31.0 0.3 convolution_add_fusion.18
  33.0 0.7 copy-done
  34.0 0.3 convolution_add_fusion.12
  35.7 0.5 multiply_convert_fusion
  36.2 3.3 %collective-permute-start.4 = (bf16[1,4,64,128]{3,2,1,0:T(8,128)(2,1)S(1)}, bf16[1,4,64,128]{3,2,1,0:T(8,128)(2,1)S(1)}, u32[]{:S(2)}, u32[]{:S(2)}) collective-permute-start(bf16[1,4,64,128]{3,2,1,0:T(8,128)(2,1)S(1)} %get-tuple-element.66), channel_id=1, source_target_pairs={{0,4},{4,8},{8,12},{1,5},{5,9},{9,13},{2,6},{6,10},{10,14},{3,7},{... | collective-permute-start | bytes 196616 | tf_op jit(solution)/shard_map/ppermute | solution.py:20
  39.5 2.1 collective-permute-start.5
  41.6 3.6 %collective-permute-done.5 = bf16[1,4,64,128]{3,2,1,0:T(8,128)(2,1)S(1)} collective-permute-done((bf16[1,4,64,128]{3,2,1,0:T(8,128)(2,1)S(1)}, bf16[1,4,64,128]{3,2,1,0:T(8,128)(2,1)S(1)}, u32[]{:S(2)}, u32[]{:S(2)}) %collective-permute-start.5) | collective-permute-done | bytes 65568 | tf_op jit(solution)/shard_map/ppermute | solution.py:22
  45.3 3.2 %collective-permute-start.6 = (bf16[6,1,64,128]{3,2,1,0:T(8,128)(2,1)S(1)}, bf16[6,1,64,128]{3,2,1,0:T(8,128)(2,1)S(1)}, u32[]{:S(2)}, u32[]{:S(2)}) collective-permute-start(bf16[6,1,64,128]{3,2,1,0:T(8,128)(2,1)S(1)} %get-tuple-element.62), channel_id=1, source_target_pairs={{0,1},{1,2},{2,3},{4,5},{5,6},{6,7},{8,9},{9,10},{10,11},{12,13},{... | collective-permute-start | bytes 294920 | tf_op jit(solution)/shard_map/ppermute | solution.py:20
  48.5 1.5 collective-permute-start.7
  50.1 3.7 %collective-permute-done.7 = bf16[6,1,64,128]{3,2,1,0:T(8,128)(2,1)S(1)} collective-permute-done((bf16[6,1,64,128]{3,2,1,0:T(8,128)(2,1)S(1)}, bf16[6,1,64,128]{3,2,1,0:T(8,128)(2,1)S(1)}, u32[]{:S(2)}, u32[]{:S(2)}) %collective-permute-start.7) | collective-permute-done | bytes 98336 | tf_op jit(solution)/shard_map/ppermute | solution.py:22
  53.9 0.7 select_maximum_fusion
  60.8 0.7 copy-done.4
  69.4 0.3 convolution_add_fusion.10
  69.7 0.3 convolution_add_fusion.9
  70.1 0.4 fusion.17
  70.4 0.3 convolution_add_fusion.7
  70.8 0.4 fusion.16
  71.2 0.4 convolution_add_fusion.5
  71.5 0.3 fusion.15
  71.9 0.3 convolution_add_fusion.3
  72.2 0.6 fusion.14
  72.8 0.3 convolution_add_fusion.1
  73.1 0.3 fusion.13
  73.5 0.3 fusion.11
  75.8 3.3 %collective-permute-start.8 = (bf16[1,6,64,128]{3,2,1,0:T(8,128)(2,1)S(1)}, bf16[1,6,64,128]{3,2,1,0:T(8,128)(2,1)S(1)}, u32[]{:S(2)}, u32[]{:S(2)}) collective-permute-start(bf16[1,6,64,128]{3,2,1,0:T(8,128)(2,1)S(1)} %get-tuple-element.57), channel_id=1, source_target_pairs={{0,4},{4,8},{8,12},{1,5},{5,9},{9,13},{2,6},{6,10},{10,14},{3,7},{... | collective-permute-start | bytes 294920 | tf_op jit(solution)/shard_map/ppermute | solution.py:32
  79.1 1.9 collective-permute-start.9
  83.1 2.0 collective-permute-done.9
  85.2 3.2 %collective-permute-start.10 = (bf16[4,1,64,128]{3,2,1,0:T(8,128)(2,1)S(1)}, bf16[4,1,64,128]{3,2,1,0:T(8,128)(2,1)S(1)}, u32[]{:S(2)}, u32[]{:S(2)}) collective-permute-start(bf16[4,1,64,128]{3,2,1,0:T(8,128)(2,1)S(1)} %get-tuple-element.61), channel_id=1, source_target_pairs={{0,1},{1,2},{2,3},{4,5},{5,6},{6,7},{8,9},{9,10},{10,11},{12,13},{... | collective-permute-start | bytes 196616 | tf_op jit(solution)/shard_map/ppermute | solution.py:32
  88.4 0.9 pad_maximum_fusion.1
  89.4 1.3 collective-permute-start.11
  90.8 3.7 %collective-permute-done.11 = bf16[4,1,64,128]{3,2,1,0:T(8,128)(2,1)S(1)} collective-permute-done((bf16[4,1,64,128]{3,2,1,0:T(8,128)(2,1)S(1)}, bf16[4,1,64,128]{3,2,1,0:T(8,128)(2,1)S(1)}, u32[]{:S(2)}, u32[]{:S(2)}) %collective-permute-start.11) | collective-permute-done | bytes 65568 | tf_op jit(solution)/shard_map/ppermute | solution.py:32
  94.5 0.3 fusion.69
  101.6 1.0 pad_maximum_fusion
  102.7 0.8 copy.43
  103.4 92.6 %all-reduce.7.cloned.1.call-done = (f32[3,3,3,58,64]{4,3,2,1,0:T(8,128)}, f32[3,3,3,64,53]{3,4,2,1,0:T(8,128)}) async-done(((f32[3,3,3,58,64]{4,3,2,1,0:T(8,128)}, f32[3,3,3,64,53]{3,4,2,1,0:T(8,128)}), (f32[3,3,3,58,64]{4,3,2,1,0:T(8,128)}, f32[3,3,3,64,53]{3,4,2,1,0:T(8,128)})) %all-reduce.7.cloned.1.call-update) | async-done | bytes 767248 | tf_op jit(solution)/shard_map/psum | solution.py:158
  196.1 2.2 %copy.200 = f32[3,3,3,58,64]{4,3,2,1,0:T(8,128)} copy(f32[3,3,3,58,64]{4,3,2,1,0:T(8,128)} %get-tuple-element.95) | data formatting | bytes 801792
  198.3 0.9 copy.201
  (168 shorter events, 31.0 us)
Async XLA Ops:
  7.2 15.7 %copy-start.3 = (bf16[3,3,3,58,64]{4,3,2,1,0:T(8,128)(2,1)S(1)}, bf16[3,3,3,58,64]{4,3,2,1,0:T(8,128)(2,1)}, u32[]{:S(2)}) copy-start(bf16[3,3,3,58,64]{4,3,2,1,0:T(8,128)(2,1)} %param.14) | copy-start | bytes 601348
  7.2 188.9 %all-reduce.7.cloned.1.call-start = ((), (), s32[]{:S(2)}) async-start(), calls=%async_computation | async-start | bytes 3317760 | tf_op jit(solution)/shard_map/psum | solution.py:158
  8.2 6.5 %collective-permute-start = (bf16[1,4,58,128]{3,2,1,0:T(8,128)(2,1)S(1)}, bf16[1,4,58,128]{3,2,1,0:T(8,128)(2,1)S(1)}, u32[]{:S(2)}, u32[]{:S(2)}) collective-permute-start(bf16[1,4,58,128]{3,2,1,0:T(8,128)(2,1)S(1)} %copy.188), channel_id=1, source_target_pairs={{0,4},{4,8},{8,12},{1,5},{5,9},{9,13},{2,6},{6,10},{10,14},{3,7},{... | collective-permute-start | bytes 178184 | tf_op jit(solution)/shard_map/ppermute | solution.py:20
  12.7 5.6 %collective-permute-start.1 = (bf16[1,4,58,128]{3,2,1,0:T(8,128)(2,1)S(1)}, bf16[1,4,58,128]{3,2,1,0:T(8,128)(2,1)S(1)}, u32[]{:S(2)}, u32[]{:S(2)}) collective-permute-start(bf16[1,4,58,128]{3,2,1,0:T(8,128)(2,1)S(1)} %copy.189), channel_id=1, source_target_pairs={{4,0},{8,4},{12,8},{5,1},{9,5},{13,9},{6,2},{10,6},{14,10},{7,3},{... | collective-permute-start | bytes 178184 | tf_op jit(solution)/shard_map/ppermute | solution.py:22
  18.4 4.8 %collective-permute-start.2 = (bf16[6,1,58,128]{3,2,1,0:T(8,128)(2,1)S(1)}, bf16[6,1,58,128]{3,2,1,0:T(8,128)(2,1)S(1)}, u32[]{:S(2)}, u32[]{:S(2)}) collective-permute-start(bf16[6,1,58,128]{3,2,1,0:T(8,128)(2,1)S(1)} %get-tuple-element.64), channel_id=1, source_target_pairs={{0,1},{1,2},{2,3},{4,5},{5,6},{6,7},{8,9},{9,10},{10,11},{12,13},{... | collective-permute-start | bytes 267272 | tf_op jit(solution)/shard_map/ppermute | solution.py:20
  21.6 5.4 %collective-permute-start.3 = (bf16[6,1,58,128]{3,2,1,0:T(8,128)(2,1)S(1)}, bf16[6,1,58,128]{3,2,1,0:T(8,128)(2,1)S(1)}, u32[]{:S(2)}, u32[]{:S(2)}) collective-permute-start(bf16[6,1,58,128]{3,2,1,0:T(8,128)(2,1)S(1)} %get-tuple-element.65), channel_id=1, source_target_pairs={{1,0},{2,1},{3,2},{5,4},{6,5},{7,6},{9,8},{10,9},{11,10},{13,12},{... | collective-permute-start | bytes 267272 | tf_op jit(solution)/shard_map/ppermute | solution.py:22
  32.8 0.9 copy-start
  36.2 5.4 %collective-permute-start.4 = (bf16[1,4,64,128]{3,2,1,0:T(8,128)(2,1)S(1)}, bf16[1,4,64,128]{3,2,1,0:T(8,128)(2,1)S(1)}, u32[]{:S(2)}, u32[]{:S(2)}) collective-permute-start(bf16[1,4,64,128]{3,2,1,0:T(8,128)(2,1)S(1)} %get-tuple-element.66), channel_id=1, source_target_pairs={{0,4},{4,8},{8,12},{1,5},{5,9},{9,13},{2,6},{6,10},{10,14},{3,7},{... | collective-permute-start | bytes 196616 | tf_op jit(solution)/shard_map/ppermute | solution.py:20
  39.5 15.0 %copy-start.1 = (bf16[3,3,3,64,53]{3,4,2,1,0:T(8,128)(2,1)S(1)}, bf16[3,3,3,64,53]{3,4,2,1,0:T(8,128)(2,1)}, u32[]{:S(2)}) copy-start(bf16[3,3,3,64,53]{3,4,2,1,0:T(8,128)(2,1)} %param.15) | copy-start | bytes 549508
  39.5 5.7 %collective-permute-start.5 = (bf16[1,4,64,128]{3,2,1,0:T(8,128)(2,1)S(1)}, bf16[1,4,64,128]{3,2,1,0:T(8,128)(2,1)S(1)}, u32[]{:S(2)}, u32[]{:S(2)}) collective-permute-start(bf16[1,4,64,128]{3,2,1,0:T(8,128)(2,1)S(1)} %get-tuple-element.67), channel_id=1, source_target_pairs={{4,0},{8,4},{12,8},{5,1},{9,5},{13,9},{6,2},{10,6},{14,10},{7,3},{... | collective-permute-start | bytes 196616 | tf_op jit(solution)/shard_map/ppermute | solution.py:22
  45.3 4.8 %collective-permute-start.6 = (bf16[6,1,64,128]{3,2,1,0:T(8,128)(2,1)S(1)}, bf16[6,1,64,128]{3,2,1,0:T(8,128)(2,1)S(1)}, u32[]{:S(2)}, u32[]{:S(2)}) collective-permute-start(bf16[6,1,64,128]{3,2,1,0:T(8,128)(2,1)S(1)} %get-tuple-element.62), channel_id=1, source_target_pairs={{0,1},{1,2},{2,3},{4,5},{5,6},{6,7},{8,9},{9,10},{10,11},{12,13},{... | collective-permute-start | bytes 294920 | tf_op jit(solution)/shard_map/ppermute | solution.py:20
  48.5 5.4 %collective-permute-start.7 = (bf16[6,1,64,128]{3,2,1,0:T(8,128)(2,1)S(1)}, bf16[6,1,64,128]{3,2,1,0:T(8,128)(2,1)S(1)}, u32[]{:S(2)}, u32[]{:S(2)}) collective-permute-start(bf16[6,1,64,128]{3,2,1,0:T(8,128)(2,1)S(1)} %get-tuple-element.63), channel_id=1, source_target_pairs={{1,0},{2,1},{3,2},{5,4},{6,5},{7,6},{9,8},{10,9},{11,10},{13,12},{... | collective-permute-start | bytes 294920 | tf_op jit(solution)/shard_map/ppermute | solution.py:22
  60.5 0.9 copy-start.4
  75.8 7.2 %collective-permute-start.8 = (bf16[1,6,64,128]{3,2,1,0:T(8,128)(2,1)S(1)}, bf16[1,6,64,128]{3,2,1,0:T(8,128)(2,1)S(1)}, u32[]{:S(2)}, u32[]{:S(2)}) collective-permute-start(bf16[1,6,64,128]{3,2,1,0:T(8,128)(2,1)S(1)} %get-tuple-element.57), channel_id=1, source_target_pairs={{0,4},{4,8},{8,12},{1,5},{5,9},{9,13},{2,6},{6,10},{10,14},{3,7},{... | collective-permute-start | bytes 294920 | tf_op jit(solution)/shard_map/ppermute | solution.py:32
  79.1 5.9 %collective-permute-start.9 = (bf16[1,6,64,128]{3,2,1,0:T(8,128)(2,1)S(1)}, bf16[1,6,64,128]{3,2,1,0:T(8,128)(2,1)S(1)}, u32[]{:S(2)}, u32[]{:S(2)}) collective-permute-start(bf16[1,6,64,128]{3,2,1,0:T(8,128)(2,1)S(1)} %get-tuple-element.56), channel_id=1, source_target_pairs={{4,0},{8,4},{12,8},{5,1},{9,5},{13,9},{6,2},{10,6},{14,10},{7,3},{... | collective-permute-start | bytes 294920 | tf_op jit(solution)/shard_map/ppermute | solution.py:32
  85.2 5.5 %collective-permute-start.10 = (bf16[4,1,64,128]{3,2,1,0:T(8,128)(2,1)S(1)}, bf16[4,1,64,128]{3,2,1,0:T(8,128)(2,1)S(1)}, u32[]{:S(2)}, u32[]{:S(2)}) collective-permute-start(bf16[4,1,64,128]{3,2,1,0:T(8,128)(2,1)S(1)} %get-tuple-element.61), channel_id=1, source_target_pairs={{0,1},{1,2},{2,3},{4,5},{5,6},{6,7},{8,9},{9,10},{10,11},{12,13},{... | collective-permute-start | bytes 196616 | tf_op jit(solution)/shard_map/ppermute | solution.py:32
  89.4 5.0 %collective-permute-start.11 = (bf16[4,1,64,128]{3,2,1,0:T(8,128)(2,1)S(1)}, bf16[4,1,64,128]{3,2,1,0:T(8,128)(2,1)S(1)}, u32[]{:S(2)}, u32[]{:S(2)}) collective-permute-start(bf16[4,1,64,128]{3,2,1,0:T(8,128)(2,1)S(1)} %get-tuple-element.60), channel_id=1, source_target_pairs={{1,0},{2,1},{3,2},{5,4},{6,5},{7,6},{9,8},{10,9},{11,10},{13,12},{... | collective-permute-start | bytes 196616 | tf_op jit(solution)/shard_map/ppermute | solution.py:32
  196.1 2.3 %copy-start.2 = (f32[3,3,3,64,53]{3,4,2,1,0:T(8,128)S(1)}, f32[3,3,3,64,53]{3,4,2,1,0:T(8,128)}, u32[]{:S(2)}) copy-start(f32[3,3,3,64,53]{3,4,2,1,0:T(8,128)} %get-tuple-element.96) | copy-start | bytes 1099012
Sparse Core Ops, SparseCore 0:
  102.8 93.2 all-reduce.6
where the time goes:
time: 208 us; the launch traced here: 206 us
  waiting for transfers between devices  112 us (54%)
  matrix products  36.2 us (17%)
  starting transfers between devices  30.7 us (15%)
  between operations  15.4 us (7%)
  local copies, waits for them, and re-layouts  7.62 us (4%)
  other arithmetic  4.08 us (2%)
    psum x1, waiting for transfers between devices, on_device(): grad_first, grad_second = lax.psum((grad_first, grad_second), ('gx', 'gy'))  92.6 us
    dot_general x54, matrix products, correlate(): jnp.einsum('xycz,co->xyoz', window, kernel[step_a, step_b, step_c], prefe...  14.4 us
    ppermute x4, starting transfers between devices, extended(): lax.ppermute(tail, axis, [(i, (i + 1) % count) for i in range(ends)])  14.2 us
    ppermute x4, waiting for transfers between devices, extended(): lax.ppermute(head, axis, [((i + 1) % count, i) for i in range(ends)])  13.6 us
    dot_general x54, matrix products, filter_grad(): jnp.einsum('xycz,xyoz->co', window, slope_term, preferred_element_type=jn...  12.7 us
    ppermute x4, starting transfers between devices, shifted(): lax.ppermute(value, axis, [(source, source + steps) for source in range(l...  9.72 us
    dot_general x27, matrix products, correlate_back(): jnp.einsum('xyoz,io->xyiz', window, kernel[step_a, step_b, step_c], prefe...  9.04 us
    ppermute x4, starting transfers between devices, extended(): lax.ppermute(head, axis, [((i + 1) % count, i) for i in range(ends)])  6.74 us
  transfers between devices with their start and end apart: 13, of which 8 were waited for; matrix products, arithmetic and copies ran while one was open for 2% of the time, Pallas kernels for 0%

commit v1 on v0

v1 whole, which is shorter than its diff:
```python
import functools
import math

import jax
import jax.numpy as jnp
from jax import lax
from jax.experimental import pallas as pl
from jax.experimental.pallas import tpu as pltpu
from jax.sharding import PartitionSpec as P

root_two_pi = 0.7978845608028654
cubic_term = 0.044715
CH = 64
bf16 = jnp.bfloat16
f32 = jnp.float32
DIRECTIONS = ((0, 1), (0, -1), (1, 0), (-1, 0), (1, 1), (1, -1), (-1, 1), (-1, -1))


def kernel(
    nx, ny, bx, by, depth, rows, normalizer,
    x_ref, t_ref, w1_ref, w2_ref, w2b_ref,
    pred_ref, g1_ref, g2_ref,
    raw_in, raw_hid, raw_grad, sh_in, sh_hid, sh_grad, wide_grad, wide_slope,
    act, acc, part, from_x, half, from_y, whole,
    halo_send, halo_recv, x_send, x_recv, y_send, y_recv, ay_send, ay_recv, ax_send, ax_recv,
):
    gx = lax.axis_index("gx")
    gy = lax.axis_index("gy")
    lanes = bx * depth
    wide = lanes + 2 * depth
    inner = slice(depth, depth + lanes)

    raw_in[...] = jnp.zeros_like(raw_in)
    raw_hid[...] = jnp.zeros_like(raw_hid)
    raw_grad[...] = jnp.zeros_like(raw_grad)
    raw_in[1 : by + 1, :, inner] = x_ref[...]

    barrier = pltpu.get_barrier_semaphore()
    for dx in range(nx):
        for dy in range(ny):
            if dx or dy:
                pl.semaphore_signal(
                    barrier,
                    inc=1,
                    device_id={"gx": lax.rem(gx + dx, nx), "gy": lax.rem(gy + dy, ny)},
                    device_id_type=pl.DeviceIdType.MESH,
                )
    pl.semaphore_wait(barrier, nx * ny - 1)

    def spans(step, count, unit):
        source = {0: (1, count), 1: (count, 1), -1: (1, 1)}[step]
        target = {0: (1, count), 1: (0, 1), -1: (count + 1, 1)}[step]
        return (
            slice(source[0] * unit, (source[0] + source[1]) * unit),
            slice(target[0] * unit, (target[0] + target[1]) * unit),
        )

    def halo(raw, slot):
        result = []
        for index, (dx, dy) in enumerate(DIRECTIONS):
            x_source, x_target = spans(dx, bx, depth)
            y_source, y_target = spans(dy, by, 1)
            to_x, to_y = gx + dx, gy + dy
            from_x_, from_y_ = gx - dx, gy - dy
            sends = (to_x >= 0) & (to_x < nx) & (to_y >= 0) & (to_y < ny)
            receives = (from_x_ >= 0) & (from_x_ < nx) & (from_y_ >= 0) & (from_y_ < ny)
            copy = pltpu.make_async_remote_copy(
                src_ref=raw.at[y_source, :, x_source],
                dst_ref=raw.at[y_target, :, x_target],
                send_sem=halo_send.at[slot, index],
                recv_sem=halo_recv.at[slot, index],
                device_id={"gx": lax.rem(to_x + nx, nx), "gy": lax.rem(to_y + ny, ny)},
                device_id_type=pl.DeviceIdType.MESH,
            )
            result.append((sends, receives, copy))
        return result

    def start(copies):
        for sends, _, copy in copies:
            pl.when(sends)(copy.start)

    def arrive(copies):
        for _, receives, copy in copies:
            pl.when(receives)(copy.wait_recv)

    def leave(copies):
        for sends, _, copy in copies:
            pl.when(sends)(copy.wait_send)

    place = lax.rem(lax.broadcasted_iota(jnp.int32, (CH, wide), 1), depth)
    first = place == 0
    last = place == depth - 1

    def shift(raw, out):
        def body(y, _):
            value = raw[y]
            out[y, CH : 2 * CH, :] = value
            full = value.astype(f32)
            out[y, :CH, :] = jnp.where(first, 0.0, pltpu.roll(full, 1, 1)).astype(bf16)
            out[y, 2 * CH :, :] = jnp.where(last, 0.0, pltpu.roll(full, wide - 1, 1)).astype(bf16)
            return 0

        lax.fori_loop(0, by + 2, body, 0)

    def conv(field, weight, y):
        block = field[pl.ds(y, 3)].reshape(9 * CH, wide)
        taps = jnp.dot(weight[...], block, preferred_element_type=f32)
        return (
            taps[:CH, :lanes]
            + taps[CH : 2 * CH, depth : depth + lanes]
            + taps[2 * CH :, 2 * depth :]
        )

    def spread(out, y, value):
        for a in range(3):
            if a:
                out[y, a * CH : (a + 1) * CH, : a * depth] = jnp.zeros((CH, a * depth), bf16)
            if a < 2:
                out[y, a * CH : (a + 1) * CH, a * depth + lanes :] = jnp.zeros(
                    (CH, (2 - a) * depth), bf16
                )
            out[y, a * CH : (a + 1) * CH, a * depth : a * depth + lanes] = value

    def filter_grad(field, terms, slot):
        acc[...] = jnp.zeros_like(acc)

        def body(y, _):
            block = field[pl.ds(y, 3)].reshape(9 * CH, wide)
            acc[...] += lax.dot_general(
                block, terms[y], (((1,), (1,)), ((), ())), preferred_element_type=f32
            )
            return 0

        lax.fori_loop(0, by, body, 0)
        used = 9 * CH
        mid = used // 2
        part[slot, :used, :] = acc[:, : 2 * CH].astype(bf16)
        part[slot, used : used + mid, :] = jnp.concatenate(
            [acc[:mid, 2 * CH :], acc[mid:, 2 * CH :]], axis=1
        ).astype(bf16)
        total = nx * ny * rows
        if total > used + mid:
            part[slot, used + mid :, :] = jnp.zeros((total - used - mid, 2 * CH), bf16)

    def remote(src, dst, send, recv, device):
        return pltpu.make_async_remote_copy(
            src_ref=src, dst_ref=dst, send_sem=send, recv_sem=recv,
            device_id=device, device_id_type=pl.DeviceIdType.MESH,
        )

    def span_x(index):
        return pl.ds(pl.multiple_of(index * (ny * rows), 16), ny * rows)

    def span_y(index):
        return pl.ds(pl.multiple_of(index * rows, 16), rows)

    def span_own():
        return pl.ds(pl.multiple_of((gx * ny + gy) * rows, 16), rows)

    def scatter_x(slot):
        copies = []
        for d in range(1, nx):
            to = lax.rem(gx + d, nx)
            copies.append(remote(
                part.at[slot, span_x(to)], from_x.at[slot, d - 1],
                x_send.at[slot, d - 1], x_recv.at[slot, d - 1], {"gx": to},
            ))
            copies[-1].start()
        return copies

    def scatter_y(slot, copies):
        total = part[slot, span_x(gx)].astype(f32)
        for d, copy in enumerate(copies):
            copy.wait_recv()
            total = total + from_x[slot, d].astype(f32)
        half[slot] = total.astype(bf16)
        result = []
        for d in range(1, ny):
            to = lax.rem(gy + d, ny)
            result.append(remote(
                half.at[slot, span_y(to)], from_y.at[slot, d - 1],
                y_send.at[slot, d - 1], y_recv.at[slot, d - 1], {"gy": to},
            ))
            result[-1].start()
        return result

    def gather_y(slot, copies):
        total = half[slot, span_y(gy)].astype(f32)
        for d, copy in enumerate(copies):
            copy.wait_recv()
            total = total + from_y[slot, d].astype(f32)
        whole[slot, span_own()] = total.astype(bf16)
        result = []
        for d in range(1, ny):
            to = lax.rem(gy + d, ny)
            result.append(remote(
                whole.at[slot, span_own()], whole.at[slot, span_own()],
                ay_send.at[slot, d - 1], ay_recv.at[slot, d - 1], {"gy": to},
            ))
            result[-1].start()
        return result

    def gather_x(slot, copies):
        for copy in copies:
            copy.wait_recv()
        result = []
        for d in range(1, nx):
            to = lax.rem(gx + d, nx)
            result.append(remote(
                whole.at[slot, span_x(gx)], whole.at[slot, span_x(gx)],
                ax_send.at[slot, d - 1], ax_recv.at[slot, d - 1], {"gx": to},
            ))
            result[-1].start()
        return result

    def finish(slot, copies, out):
        for copy in copies:
            copy.wait_recv()
        used = 9 * CH
        mid = used // 2
        both = whole[slot, :used, :].astype(f32)
        out[0] = both[:, :CH]
        out[1] = both[:, CH:]
        rest = whole[slot, used : used + mid, :].astype(f32)
        out[2, :mid, :] = rest[:, :CH]
        out[2, mid:, :] = rest[:, CH:]

    in_copies = halo(raw_in, 0)
    start(in_copies)
    arrive(in_copies)
    shift(raw_in, sh_in)

    def first_layer(y, _):
        value = conv(sh_in, w1_ref, y)
        act[y] = value
        tangent = jnp.tanh(root_two_pi * (value + cubic_term * value * value * value))
        raw_hid[y + 1, :, inner] = (0.5 * value * (1.0 + tangent)).astype(bf16)
        return 0

    lax.fori_loop(0, by, first_layer, 0)
    hid_copies = halo(raw_hid, 1)
    start(hid_copies)

    def slopes(y, _):
        value = act[y]
        tangent = jnp.tanh(root_two_pi * (value + cubic_term * value * value * value))
        act[y] = 0.5 * (1.0 + tangent) + 0.5 * value * (
            1.0 - tangent * tangent
        ) * root_two_pi * (1.0 + 3.0 * cubic_term * value * value)
        return 0

    lax.fori_loop(0, by, slopes, 0)
    arrive(hid_copies)
    shift(raw_hid, sh_hid)

    def second_layer(y, _):
        value = conv(sh_hid, w2_ref, y)
        pred_ref[y] = value.astype(bf16)
        grad = ((value - t_ref[y].astype(f32)) * normalizer).astype(bf16)
        raw_grad[y + 1, :, inner] = grad
        spread(wide_grad, y, grad)
        return 0

    lax.fori_loop(0, by, second_layer, 0)
    grad_copies = halo(raw_grad, 2)
    start(grad_copies)
    filter_grad(sh_hid, wide_grad, 1)
    scatter_x_second = scatter_x(1)
    arrive(grad_copies)
    shift(raw_grad, sh_grad)

    def back(y, _):
        value = conv(sh_grad, w2b_ref, y)
        spread(wide_slope, y, (value * act[y]).astype(bf16))
        return 0

    lax.fori_loop(0, by, back, 0)
    scatter_y_second = scatter_y(1, scatter_x_second)
    filter_grad(sh_in, wide_slope, 0)
    scatter_x_first = scatter_x(0)
    gather_y_second = gather_y(1, scatter_y_second)
    scatter_y_first = scatter_y(0, scatter_x_first)
    gather_x_second = gather_x(1, gather_y_second)
    gather_y_first = gather_y(0, scatter_y_first)
    finish(1, gather_x_second, g2_ref)
    gather_x_first = gather_x(0, gather_y_first)
    finish(0, gather_x_first, g1_ref)

    for copies in (in_copies, hid_copies, grad_copies):
        leave(copies)
    for copies in (
        scatter_x_second, scatter_y_second, gather_y_second, gather_x_second,
        scatter_x_first, scatter_y_first, gather_y_first, gather_x_first,
    ):
        for copy in copies:
            copy.wait_send()


def on_device(nx, ny, inputs, target, w_first, w_second):
    bx, by, cin, depth = inputs.shape
    cout = target.shape[2]
    hid = w_first.shape[4]
    normalizer = 1.0 / math.sqrt(bx * nx * by * ny * depth)
    used = 9 * CH * 3 // 2
    rows = -(-used // (nx * ny * 16)) * 16

    def flat(field):
        padded = jnp.pad(field, ((0, 0), (0, 0), (0, CH - field.shape[2]), (0, 0)))
        return padded.transpose(1, 2, 0, 3).reshape(by, CH, bx * depth)

    def weights(w, order):
        w = jnp.pad(w, ((0, 0),) * 3 + ((0, CH - w.shape[3]), (0, CH - w.shape[4])))
        return w.transpose(order).reshape(3 * CH, 9 * CH)

    forward = (0, 4, 1, 2, 3)
    lanes = bx * depth
    wide = lanes + 2 * depth
    vmem = pl.BlockSpec(memory_space=pltpu.VMEM)
    total = nx * ny * rows
    dma = pltpu.SemaphoreType.DMA
    macs = 5 * 192 * 576 * wide * by
    prediction, g1, g2 = pl.pallas_call(
        functools.partial(kernel, nx, ny, bx, by, depth, rows, normalizer),
        out_shape=(
            jax.ShapeDtypeStruct((by, CH, lanes), bf16),
            jax.ShapeDtypeStruct((3, 9 * CH, CH), f32),
            jax.ShapeDtypeStruct((3, 9 * CH, CH), f32),
        ),
        in_specs=[vmem] * 5,
        out_specs=(vmem,) * 3,
        scratch_shapes=(
            [pltpu.VMEM((by + 2, CH, wide), bf16)] * 3
            + [pltpu.VMEM((by + 2, 3 * CH, wide), bf16)] * 3
            + [pltpu.VMEM((by, 3 * CH, wide), bf16)] * 2
            + [
                pltpu.VMEM((by, CH, lanes), f32),
                pltpu.VMEM((9 * CH, 3 * CH), f32),
                pltpu.VMEM((2, total, 2 * CH), bf16),
                pltpu.VMEM((2, nx - 1, ny * rows, 2 * CH), bf16),
                pltpu.VMEM((2, ny * rows, 2 * CH), bf16),
                pltpu.VMEM((2, ny - 1, rows, 2 * CH), bf16),
                pltpu.VMEM((2, total, 2 * CH), bf16),
                dma((3, 8)), dma((3, 8)),
                dma((2, nx - 1)), dma((2, nx - 1)),
                dma((2, ny - 1)), dma((2, ny - 1)),
                dma((2, ny - 1)), dma((2, ny - 1)),
                dma((2, nx - 1)), dma((2, nx - 1)),
            ]
        ),
        compiler_params=pltpu.CompilerParams(
            collective_id=0, has_side_effects=True, vmem_limit_bytes=48 * 1024 * 1024
        ),
        cost_estimate=pl.CostEstimate(
            flops=2 * macs, bytes_accessed=8 * 2**20, transcendentals=2 * by * CH * lanes
        ),
    )(
        flat(inputs),
        flat(target),
        weights(w_first, forward),
        weights(w_second, forward),
        weights(w_second[::-1, ::-1, ::-1], (0, 3, 1, 2, 4)),
    )
    prediction = prediction.reshape(by, CH, bx, depth).transpose(2, 0, 1, 3)[:, :, :cout]
    g1 = g1.reshape(3, 3, 3, CH, CH)[:, :, :, :cin, :hid]
    g2 = g2.reshape(3, 3, 3, CH, CH)[:, :, :, :hid, :cout]
    return prediction, g1, g2


def solution(mesh):
    placed = (
        P(("groups", "gx"), "gy", None, None),
        P(("groups", "gx"), "gy", None, None),
        P(),
        P(),
    )
    return jax.shard_map(
        functools.partial(on_device, mesh.shape["gx"], mesh.shape["gy"]),
        mesh=mesh,
        in_specs=placed,
        out_specs=(
            P(("groups", "gx"), "gy", None, None),
            P("groups", None, None, None, None),
            P("groups", None, None, None, None),
        ),
        check_vma=False,
    )
```

time: 208 us -> 54.8 us (0.26)
  waiting for transfers between devices: 112 us -> 0 us
  Pallas kernels: 0 us -> 42.7 us
  matrix products: 36.2 us -> 0 us
  starting transfers between devices: 30.7 us -> 0 us
  between operations: 15.4 us -> 0.78 us
  other arithmetic: 4.08 us -> 0 us
  local copies, waits for them, and re-layouts: 7.62 us -> 11.1 us
    psum x1 -> x0, waiting for transfers between devices: 92.6 us -> none  [on_device(): grad_first, grad_second = lax.psum((grad_first, grad_second), ('gx', 'gy'))]
    pallas_call x0 -> x1, Pallas kernels: none -> 42.7 us  [on_device(): pl.pallas_call(functools.partial(kernel, nx, ny, bx, by, depth, rows, nor...]
    dot_general x135 -> x0, matrix products: 36.2 us -> none  [the longest x54 14.4 us: correlate(): jnp.einsum('xycz,co->xyoz', window, kernel[step_a, step_b, step_c], prefe...]
    ppermute x12 -> x0, starting transfers between devices: 30.7 us -> none  [the longest x4 14.2 us: extended(): lax.ppermute(tail, axis, [(i, (i + 1) % count) for i in range(ends)])]
    ppermute x12 -> x0, waiting for transfers between devices: 19.4 us -> none  [the longest x4 13.6 us: extended(): lax.ppermute(head, axis, [((i + 1) % count, i) for i in range(ends)])]
    transpose x0 -> x10, local copies, waits for them, and re-layouts: none -> 4.16 us  [the longest x6 2.59 us: weights(): return w.transpose(order).reshape(3 * CH, 9 * CH)]
    another operation x21 -> x0, other arithmetic: 2.35 us -> none  [the longest x8 2.1 us: filter_grad(): return jnp.stack(planes)]
    unnamed x17 -> x8, local copies, waits for them, and re-layouts: 6.51 us -> 4.44 us
  transfers between devices with their start and end apart: 13 -> 0, of which waited for: 8 -> 0; matrix products, arithmetic and copies ran while one was open for 2% -> 0% of each run, Pallas kernels for 0% -> 0%
where the time goes in v1:
time: 54.8 us; the launch traced here: 54.5 us
  Pallas kernels  42.7 us (78%)
  local copies, waits for them, and re-layouts  11.1 us (20%)
  between operations  0.78 us (1%)
    pallas_call x1, Pallas kernels, on_device(): pl.pallas_call(functools.partial(kernel, nx, ny, bx, by, depth, rows, nor...  42.7 us
    unnamed x8, local copies, waits for them, and re-layouts  4.44 us
    transpose x6, local copies, waits for them, and re-layouts, weights(): return w.transpose(order).reshape(3 * CH, 9 * CH)  2.59 us
    transpose x4, local copies, waits for them, and re-layouts, flat(): return padded.transpose(1, 2, 0, 3).reshape(by, CH, bx * depth)  1.58 us
    reshape x3, local copies, waits for them, and re-layouts, weights(): return w.transpose(order).reshape(3 * CH, 9 * CH)  1.18 us

profile of v1, /device:TPU:1, one launch (start us, length us, event | category | flops | bytes accessed | tf_op | source)
XLA Modules:
  0.0 54.5 jit_solution(296993964461157004)
XLA Ops:
  0.6 1.1 %pad_bitcast_fusion.4 = bf16[4,64,4,128]{3,0,1,2:T(4,128)(2,1)S(1)} fusion(bf16[4,4,58,128]{3,1,2,0:T(4,128)(2,1)} %param.4), kind=kLoop, calls=%fused_computation.5 | loop fusion | bytes 499712 | tf_op jit(solution)/shard_map/transpose | solution.py:309
  1.7 0.2 copy.14
  1.9 0.0 copy-start.2
  1.9 0.1 reshape.30.x_ref
  2.0 0.8 %copy-done.2 = bf16[4,4,53,128]{3,1,2,0:T(4,128)(2,1)S(1)} copy-done((bf16[4,4,53,128]{3,1,2,0:T(4,128)(2,1)S(1)}, bf16[4,4,53,128]{3,1,2,0:T(4,128)(2,1)}, u32[]{:S(2)}) %copy-start.2) | copy-done | bytes 217112
  2.8 0.1 pad_bitcast_fusion.3
  3.0 0.2 copy.15
  3.2 0.0 copy-start
  3.2 0.1 reshape.31.t_ref
  3.3 0.9 %copy-done = bf16[3,3,3,64,53]{3,4,2,1,0:T(8,128)(2,1)S(1)} copy-done((bf16[3,3,3,64,53]{3,4,2,1,0:T(8,128)(2,1)S(1)}, bf16[3,3,3,64,53]{3,4,2,1,0:T(8,128)(2,1)}, u32[]{:S(2)}) %copy-start) | copy-done | bytes 183192
  4.2 0.1 pad_bitcast_fusion
  4.3 0.9 %copy.18 = bf16[3,64,3,3,64]{4,3,2,1,0:T(4,128)(2,1)S(1)} copy(bf16[3,64,3,3,64]{1,4,3,2,0:T(8,128)(2,1)S(1)} %pad_bitcast_fusion) | data formatting | bytes 442368 | tf_op jit(solution)/shard_map/transpose | solution.py:313
  5.3 0.0 copy-start.1
  5.3 0.4 reshape.34.w2b_ref
  5.7 0.6 %copy-done.1 = bf16[3,3,3,58,64]{4,3,2,1,0:T(8,128)(2,1)S(1)} copy-done((bf16[3,3,3,58,64]{4,3,2,1,0:T(8,128)(2,1)S(1)}, bf16[3,3,3,58,64]{4,3,2,1,0:T(8,128)(2,1)}, u32[]{:S(2)}) %copy-start.1) | copy-done | bytes 200472
  6.3 0.1 pad_bitcast_fusion.2
  6.4 0.9 %copy.16 = bf16[3,64,3,3,64]{4,3,2,1,0:T(4,128)(2,1)S(1)} copy(bf16[3,64,3,3,64]{1,4,3,2,0:T(8,128)(2,1)S(1)} %pad_bitcast_fusion.2) | data formatting | bytes 442368 | tf_op jit(solution)/shard_map/transpose | solution.py:313
  7.3 0.4 reshape.32.w1_ref
  7.7 0.1 pad_bitcast_fusion.1
  7.9 0.4 copy.17
  8.2 0.4 reshape.33.w2_ref
  8.6 42.7 %shard_map.67 = (bf16[4,64,512]{2,1,0:T(8,128)(2,1)S(1)}, f32[3,576,64]{2,1,0:T(8,128)S(1)}, f32[3,576,64]{2,1,0:T(8,128)S(1)}) custom-call(bf16[4,64,512]{2,1,0:T(8,128)(2,1)S(1)} %reshape.30.x_ref, bf16[4,64,512]{2,1,0:T(8,128)(2,1)S(1)} %reshape.31.t_ref, bf16[192,576]{1,0:T(8,128)(2,1)S(1)} %reshape.32.w1_ref, bf16[192,576]{1,0:T(8,128)(2,1)S(1)} %reshape.33.w2_ref, ...), custom_call_target="tpu_custom_call" | custom-call | flops 3397386240 | bytes 8388608 | tf_op jit(solution)/shard_map/pallas_call | solution.py:322
  51.3 0.1 reshape.35
  51.4 0.2 copy.23
  51.6 0.8 %slice.12 = bf16[4,4,53,128]{3,1,2,0:T(4,128)(2,1)} slice(bf16[4,4,64,128]{3,1,2,0:T(4,128)(2,1)S(1)} %bitcast.19), slice={[0:4], [0:4], [0:53], [0:128]} | slice | bytes 434176 | tf_op jit(solution)/shard_map/slice | solution.py:363
  52.4 1.2 %copy.21 = f32[3,3,3,64,53]{3,4,2,1,0:T(8,128)} copy(f32[3,3,3,64,53]{4,3,2,1,0:T(8,128)S(1)} %bitcast.18) | data formatting | bytes 732672
  53.6 0.9 %copy.25 = f32[3,3,3,58,64]{4,3,2,1,0:T(8,128)} copy(f32[3,3,3,58,64]{4,3,2,1,0:T(8,128)S(1)} %bitcast.17) | data formatting | bytes 801792
  (1 shorter events, 0.0 us)
Async XLA Ops:
  1.9 0.9 %copy-start.2 = (bf16[4,4,53,128]{3,1,2,0:T(4,128)(2,1)S(1)}, bf16[4,4,53,128]{3,1,2,0:T(4,128)(2,1)}, u32[]{:S(2)}) copy-start(bf16[4,4,53,128]{3,1,2,0:T(4,128)(2,1)} %param.5) | copy-start | bytes 651268
  3.2 1.0 %copy-start = (bf16[3,3,3,64,53]{3,4,2,1,0:T(8,128)(2,1)S(1)}, bf16[3,3,3,64,53]{3,4,2,1,0:T(8,128)(2,1)}, u32[]{:S(2)}) copy-start(bf16[3,3,3,64,53]{3,4,2,1,0:T(8,128)(2,1)} %param.7) | copy-start | bytes 549508
  5.3 1.0 %copy-start.1 = (bf16[3,3,3,58,64]{4,3,2,1,0:T(8,128)(2,1)S(1)}, bf16[3,3,3,58,64]{4,3,2,1,0:T(8,128)(2,1)}, u32[]{:S(2)}) copy-start(bf16[3,3,3,58,64]{4,3,2,1,0:T(8,128)(2,1)} %param.6) | copy-start | bytes 601348

commit v2 on v1

--- a/solution.py
+++ b/solution.py
@@ -18,22 +18,24 @@
 
 def kernel(
     nx, ny, bx, by, depth, rows, normalizer,
-    x_ref, t_ref, w1_ref, w2_ref, w2b_ref,
+    x_ref, t_ref, w1_ref, w2_ref,
     pred_ref, g1_ref, g2_ref,
     raw_in, raw_hid, raw_grad, sh_in, sh_hid, sh_grad, wide_grad, wide_slope,
-    act, acc, part, from_x, half, from_y, whole,
+    first_w, second_w, back_w, act, acc, part, from_x, half, from_y, whole,
     halo_send, halo_recv, x_send, x_recv, y_send, y_recv, ay_send, ay_recv, ax_send, ax_recv,
 ):
     gx = lax.axis_index("gx")
     gy = lax.axis_index("gy")
-    lanes = bx * depth
+    lanes = by * depth
     wide = lanes + 2 * depth
     inner = slice(depth, depth + lanes)
 
-    raw_in[...] = jnp.zeros_like(raw_in)
-    raw_hid[...] = jnp.zeros_like(raw_hid)
-    raw_grad[...] = jnp.zeros_like(raw_grad)
-    raw_in[1 : by + 1, :, inner] = x_ref[...]
+    for raw in (raw_in, raw_hid, raw_grad):
+        raw[0] = jnp.zeros((CH, wide), bf16)
+        raw[bx + 1] = jnp.zeros((CH, wide), bf16)
+        raw[1 : bx + 1, :, :depth] = jnp.zeros((bx, CH, depth), bf16)
+        raw[1 : bx + 1, :, depth + lanes :] = jnp.zeros((bx, CH, depth), bf16)
+    raw_in[1 : bx + 1, :, inner] = x_ref[...]
 
     barrier = pltpu.get_barrier_semaphore()
     for dx in range(nx):
@@ -58,15 +60,15 @@
     def halo(raw, slot):
         result = []
         for index, (dx, dy) in enumerate(DIRECTIONS):
-            x_source, x_target = spans(dx, bx, depth)
-            y_source, y_target = spans(dy, by, 1)
+            x_source, x_target = spans(dx, bx, 1)
+            y_source, y_target = spans(dy, by, depth)
             to_x, to_y = gx + dx, gy + dy
             from_x_, from_y_ = gx - dx, gy - dy
             sends = (to_x >= 0) & (to_x < nx) & (to_y >= 0) & (to_y < ny)
             receives = (from_x_ >= 0) & (from_x_ < nx) & (from_y_ >= 0) & (from_y_ < ny)
             copy = pltpu.make_async_remote_copy(
-                src_ref=raw.at[y_source, :, x_source],
-                dst_ref=raw.at[y_target, :, x_target],
+                src_ref=raw.at[x_source, :, y_source],
+                dst_ref=raw.at[x_target, :, y_target],
                 send_sem=halo_send.at[slot, index],
                 recv_sem=halo_recv.at[slot, index],
                 device_id={"gx": lax.rem(to_x + nx, nx), "gy": lax.rem(to_y + ny, ny)},
@@ -92,18 +94,18 @@
     last = place == depth - 1
 
     def shift(raw, out):
-        def body(y, _):
-            value = raw[y]
-            out[y, CH : 2 * CH, :] = value
+        def body(x, _):
+            value = raw[x]
+            out[x, CH : 2 * CH, :] = value
             full = value.astype(f32)
-            out[y, :CH, :] = jnp.where(first, 0.0, pltpu.roll(full, 1, 1)).astype(bf16)
-            out[y, 2 * CH :, :] = jnp.where(last, 0.0, pltpu.roll(full, wide - 1, 1)).astype(bf16)
+            out[x, :CH, :] = jnp.where(first, 0.0, pltpu.roll(full, 1, 1)).astype(bf16)
+            out[x, 2 * CH :, :] = jnp.where(last, 0.0, pltpu.roll(full, wide - 1, 1)).astype(bf16)
             return 0
 
-        lax.fori_loop(0, by + 2, body, 0)
-
-    def conv(field, weight, y):
-        block = field[pl.ds(y, 3)].reshape(9 * CH, wide)
+        lax.fori_loop(0, bx + 2, body, 0)
+
+    def conv(field, weight, x):
+        block = field[pl.ds(x, 3)].reshape(9 * CH, wide)
         taps = jnp.dot(weight[...], block, preferred_element_type=f32)
         return (
             taps[:CH, :lanes]
@@ -111,27 +113,27 @@
             + taps[2 * CH :, 2 * depth :]
         )
 
-    def spread(out, y, value):
+    def spread(out, x, value):
         for a in range(3):
             if a:
-                out[y, a * CH : (a + 1) * CH, : a * depth] = jnp.zeros((CH, a * depth), bf16)
+                out[x, a * CH : (a + 1) * CH, : a * depth] = jnp.zeros((CH, a * depth), bf16)
             if a < 2:
-                out[y, a * CH : (a + 1) * CH, a * depth + lanes :] = jnp.zeros(
+                out[x, a * CH : (a + 1) * CH, a * depth + lanes :] = jnp.zeros(
                     (CH, (2 - a) * depth), bf16
                 )
-            out[y, a * CH : (a + 1) * CH, a * depth : a * depth + lanes] = value
+            out[x, a * CH : (a + 1) * CH, a * depth : a * depth + lanes] = value
 
     def filter_grad(field, terms, slot):
         acc[...] = jnp.zeros_like(acc)
 
-        def body(y, _):
-            block = field[pl.ds(y, 3)].reshape(9 * CH, wide)
+        def body(x, _):
+            block = field[pl.ds(x, 3)].reshape(9 * CH, wide)
             acc[...] += lax.dot_general(
-                block, terms[y], (((1,), (1,)), ((), ())), preferred_element_type=f32
+                block, terms[x], (((1,), (1,)), ((), ())), preferred_element_type=f32
             )
             return 0
 
-        lax.fori_loop(0, by, body, 0)
+        lax.fori_loop(0, bx, body, 0)
         used = 9 * CH
         mid = used // 2
         part[slot, :used, :] = acc[:, : 2 * CH].astype(bf16)
@@ -219,49 +221,67 @@
         used = 9 * CH
         mid = used // 2
         both = whole[slot, :used, :].astype(f32)
-        out[0] = both[:, :CH]
-        out[1] = both[:, CH:]
         rest = whole[slot, used : used + mid, :].astype(f32)
-        out[2, :mid, :] = rest[:, :CH]
-        out[2, mid:, :] = rest[:, CH:]
+        rest = jnp.concatenate([rest[:, :CH], rest[:, CH:]], axis=0)
+        third = 3 * CH
+        for a in range(3):
+            out[a, 0] = both[a * third : (a + 1) * third, :CH]
+            out[a, 1] = both[a * third : (a + 1) * third, CH:]
+            out[a, 2] = rest[a * third : (a + 1) * third]
+
+    def turned(blocks):
+        stacked = jnp.concatenate([block.astype(f32) for block in blocks], axis=0)
+        return stacked.T.astype(bf16)
 
     in_copies = halo(raw_in, 0)
     start(in_copies)
+    for b in range(3):
+        first_w[b * CH : (b + 1) * CH, :] = turned(
+            [w1_ref[(a * 3 + b) * 3 + c] for a in range(3) for c in range(3)]
+        )
+        for a in range(3):
+            for c in range(3):
+                column = (a * 3 + c) * CH
+                second_w[b * CH : (b + 1) * CH, column : column + CH] = w2_ref[(a * 3 + b) * 3 + c]
     arrive(in_copies)
     shift(raw_in, sh_in)
 
-    def first_layer(y, _):
-        value = conv(sh_in, w1_ref, y)
-        act[y] = value
+    def first_layer(x, _):
+        value = conv(sh_in, first_w, x)
+        act[x] = value
         tangent = jnp.tanh(root_two_pi * (value + cubic_term * value * value * value))
-        raw_hid[y + 1, :, inner] = (0.5 * value * (1.0 + tangent)).astype(bf16)
+        raw_hid[x + 1, :, inner] = (0.5 * value * (1.0 + tangent)).astype(bf16)
         return 0
 
-    lax.fori_loop(0, by, first_layer, 0)
+    lax.fori_loop(0, bx, first_layer, 0)
     hid_copies = halo(raw_hid, 1)
     start(hid_copies)
-
-    def slopes(y, _):
-        value = act[y]
+    for b in range(3):
+        back_w[b * CH : (b + 1) * CH, :] = turned(
+            [w2_ref[((2 - a) * 3 + 2 - b) * 3 + 2 - c] for a in range(3) for c in range(3)]
+        )
+
+    def slopes(x, _):
+        value = act[x]
         tangent = jnp.tanh(root_two_pi * (value + cubic_term * value * value * value))
-        act[y] = 0.5 * (1.0 + tangent) + 0.5 * value * (
+        act[x] = 0.5 * (1.0 + tangent) + 0.5 * value * (
             1.0 - tangent * tangent
         ) * root_two_pi * (1.0 + 3.0 * cubic_term * value * value)
         return 0
 
-    lax.fori_loop(0, by, slopes, 0)
+    lax.fori_loop(0, bx, slopes, 0)
     arrive(hid_copies)
     shift(raw_hid, sh_hid)
 
-    def second_layer(y, _):
-        value = conv(sh_hid, w2_ref, y)
-        pred_ref[y] = value.astype(bf16)
-        grad = ((value - t_ref[y].astype(f32)) * normalizer).astype(bf16)
-        raw_grad[y + 1, :, inner] = grad
-        spread(wide_grad, y, grad)
+    def second_layer(x, _):
+        value = conv(sh_hid, second_w, x)
+        pred_ref[x] = value.astype(bf16)
+        grad = ((value - t_ref[x].astype(f32)) * normalizer).astype(bf16)
+        raw_grad[x + 1, :, inner] = grad
+        spread(wide_grad, x, grad)
         return 0
 
-    lax.fori_loop(0, by, second_layer, 0)
+    lax.fori_loop(0, bx, second_layer, 0)
     grad_copies = halo(raw_grad, 2)
     start(grad_copies)
     filter_grad(sh_hid, wide_grad, 1)
@@ -269,12 +289,12 @@
     arrive(grad_copies)
     shift(raw_grad, sh_grad)
 
-    def back(y, _):
-        value = conv(sh_grad, w2b_ref, y)
-        spread(wide_slope, y, (value * act[y]).astype(bf16))
+    def back(x, _):
+        value = conv(sh_grad, back_w, x)
+        spread(wide_slope, x, (value * act[x]).astype(bf16))
         return 0
 
-    lax.fori_loop(0, by, back, 0)
+    lax.fori_loop(0, bx, back, 0)
     scatter_y_second = scatter_y(1, scatter_x_second)
     filter_grad(sh_in, wide_slope, 0)
     scatter_x_first = scatter_x(0)
@@ -305,35 +325,35 @@
     rows = -(-used // (nx * ny * 16)) * 16
 
     def flat(field):
-        padded = jnp.pad(field, ((0, 0), (0, 0), (0, CH - field.shape[2]), (0, 0)))
-        return padded.transpose(1, 2, 0, 3).reshape(by, CH, bx * depth)
-
-    def weights(w, order):
+        rolled = field.transpose(0, 2, 1, 3).reshape(bx, field.shape[2], by * depth)
+        return jnp.pad(rolled, ((0, 0), (0, CH - field.shape[2]), (0, 0)))
+
+    def taps(w):
         w = jnp.pad(w, ((0, 0),) * 3 + ((0, CH - w.shape[3]), (0, CH - w.shape[4])))
-        return w.transpose(order).reshape(3 * CH, 9 * CH)
-
-    forward = (0, 4, 1, 2, 3)
-    lanes = bx * depth
+        return w.reshape(27, CH, CH)
+
+    lanes = by * depth
     wide = lanes + 2 * depth
     vmem = pl.BlockSpec(memory_space=pltpu.VMEM)
     total = nx * ny * rows
     dma = pltpu.SemaphoreType.DMA
-    macs = 5 * 192 * 576 * wide * by
+    macs = 5 * 192 * 576 * wide * bx
     prediction, g1, g2 = pl.pallas_call(
         functools.partial(kernel, nx, ny, bx, by, depth, rows, normalizer),
         out_shape=(
-            jax.ShapeDtypeStruct((by, CH, lanes), bf16),
-            jax.ShapeDtypeStruct((3, 9 * CH, CH), f32),
-            jax.ShapeDtypeStruct((3, 9 * CH, CH), f32),
+            jax.ShapeDtypeStruct((bx, CH, lanes), bf16),
+            jax.ShapeDtypeStruct((3, 3, 3 * CH, CH), f32),
+            jax.ShapeDtypeStruct((3, 3, 3 * CH, CH), f32),
         ),
-        in_specs=[vmem] * 5,
+        in_specs=[vmem] * 4,
         out_specs=(vmem,) * 3,
         scratch_shapes=(
-            [pltpu.VMEM((by + 2, CH, wide), bf16)] * 3
-            + [pltpu.VMEM((by + 2, 3 * CH, wide), bf16)] * 3
-            + [pltpu.VMEM((by, 3 * CH, wide), bf16)] * 2
+            [pltpu.VMEM((bx + 2, CH, wide), bf16)] * 3
+            + [pltpu.VMEM((bx + 2, 3 * CH, wide), bf16)] * 3
+            + [pltpu.VMEM((bx, 3 * CH, wide), bf16)] * 2
+            + [pltpu.VMEM((3 * CH, 9 * CH), bf16)] * 3
             + [
-                pltpu.VMEM((by, CH, lanes), f32),
+                pltpu.VMEM((bx, CH, lanes), f32),
                 pltpu.VMEM((9 * CH, 3 * CH), f32),
                 pltpu.VMEM((2, total, 2 * CH), bf16),
                 pltpu.VMEM((2, nx - 1, ny * rows, 2 * CH), bf16),
@@ -351,16 +371,15 @@
             collective_id=0, has_side_effects=True, vmem_limit_bytes=48 * 1024 * 1024
         ),
         cost_estimate=pl.CostEstimate(
-            flops=2 * macs, bytes_accessed=8 * 2**20, transcendentals=2 * by * CH * lanes
+            flops=2 * macs, bytes_accessed=8 * 2**20, transcendentals=2 * bx * CH * lanes
         ),
     )(
         flat(inputs),
         flat(target),
-        weights(w_first, forward),
-        weights(w_second, forward),
-        weights(w_second[::-1, ::-1, ::-1], (0, 3, 1, 2, 4)),
+        taps(w_first),
+        taps(w_second.transpose(0, 1, 2, 4, 3)),
     )
-    prediction = prediction.reshape(by, CH, bx, depth).transpose(2, 0, 1, 3)[:, :, :cout]
+    prediction = prediction.reshape(bx, CH, by, depth)[:, :cout].transpose(0, 2, 1, 3)
     g1 = g1.reshape(3, 3, 3, CH, CH)[:, :, :, :cin, :hid]
     g2 = g2.reshape(3, 3, 3, CH, CH)[:, :, :, :hid, :cout]
     return prediction, g1, g2

time: 54.8 us -> 50.6 us (0.923)
  local copies, waits for them, and re-layouts: 11.1 us -> 7.01 us
    transpose x10 -> x1, local copies, waits for them, and re-layouts: 4.16 us -> 0.76 us  [on_device(): prediction.reshape(bx, CH, by, depth)[:, :cout].transpose(0, 2, 1, 3)]
    slice x1 -> x0, local copies, waits for them, and re-layouts: 0.76 us -> none  [on_device(): prediction.reshape(by, CH, bx, depth).transpose(2, 0, 1, 3)[:, :, :cout]]
    reshape x7 -> x3, local copies, waits for them, and re-layouts: 1.66 us -> 1.18 us  [the longest x2 1.12 us: flat(): rolled = field.transpose(0, 2, 1, 3).reshape(bx, field.shape[2], by * depth)]
where the time goes in v2:
time: 50.6 us; the launch traced here: 50.3 us
  Pallas kernels  42.6 us (84%)
  local copies, waits for them, and re-layouts  7.01 us (14%)
  between operations  0.69 us (1%)
    pallas_call x1, Pallas kernels, on_device(): pl.pallas_call(functools.partial(kernel, nx, ny, bx, by, depth, rows, nor...  42.6 us
    unnamed x8, local copies, waits for them, and re-layouts  4.8 us
    reshape x2, local copies, waits for them, and re-layouts, flat(): rolled = field.transpose(0, 2, 1, 3).reshape(bx, field.shape[2], by * depth)  1.12 us

profile of v2, /device:TPU:1, one launch (start us, length us, event | category | flops | bytes accessed | tf_op | source)
XLA Modules:
  0.0 50.3 jit_solution(4019872951130284173)
XLA Ops:
  0.6 1.0 %reshape.28 = bf16[4,53,512]{2,1,0:T(8,128)(2,1)S(1)} reshape(bf16[4,53,4,128]{3,2,1,0:T(4,128)(2,1)} %bitcast.17) | data formatting | bytes 434176 | tf_op jit(solution)/shard_map/reshape | solution.py:328
  1.7 0.0 copy-start.2
  1.7 0.9 %copy-done.2 = bf16[4,4,58,128]{3,1,2,0:T(4,128)(2,1)S(1)} copy-done((bf16[4,4,58,128]{3,1,2,0:T(4,128)(2,1)S(1)}, bf16[4,4,58,128]{3,1,2,0:T(4,128)(2,1)}, u32[]{:S(2)}) %copy-start.2) | copy-done | bytes 237592
  2.6 0.0 copy-start
  2.6 0.1 reshape.34
  2.7 0.9 %copy-done = bf16[3,3,3,58,64]{4,3,2,1,0:T(8,128)(2,1)S(1)} copy-done((bf16[3,3,3,58,64]{4,3,2,1,0:T(8,128)(2,1)S(1)}, bf16[3,3,3,58,64]{4,3,2,1,0:T(8,128)(2,1)}, u32[]{:S(2)}) %copy-start) | copy-done | bytes 200472
  3.6 0.0 copy-start.1
  3.6 0.1 pad.18
  3.7 0.9 %copy-done.1 = bf16[3,3,3,64,53]{3,4,2,1,0:T(8,128)(2,1)S(1)} copy-done((bf16[3,3,3,64,53]{3,4,2,1,0:T(8,128)(2,1)S(1)}, bf16[3,3,3,64,53]{3,4,2,1,0:T(8,128)(2,1)}, u32[]{:S(2)}) %copy-start.1) | copy-done | bytes 183192
  4.6 0.1 pad.19
  4.7 42.6 %shard_map.67 = (bf16[4,64,512]{2,1,0:T(8,128)(2,1)S(1)}, f32[3,3,192,64]{3,2,1,0:T(8,128)S(1)}, f32[3,3,192,64]{3,2,1,0:T(8,128)S(1)}) custom-call(bf16[4,64,512]{2,1,0:T(8,128)(2,1)S(1)} %pad.16.x_ref, bf16[4,64,512]{2,1,0:T(8,128)(2,1)S(1)} %pad.17.t_ref, bf16[27,64,64]{2,1,0:T(8,128)(2,1)S(1)} %bitcast.13, bf16[27,64,64]{2,1,0:T(8,128)(2,1)S(1)} %bitcast.14), custom_call_target="tpu_custom_call" | custom-call | flops 3397386240 | bytes 8388608 | tf_op jit(solution)/shard_map/pallas_call | solution.py:341
  47.4 0.1 reshape.31
  47.4 0.8 %slice_bitcast_fusion = bf16[4,4,53,128]{3,1,2,0:T(4,128)(2,1)} fusion(bf16[4,64,4,128]{3,2,1,0:T(4,128)(2,1)S(1)} %reshape.31), kind=kLoop, calls=%fused_computation | loop fusion | bytes 434176 | tf_op jit(solution)/shard_map/transpose | solution.py:382
  48.2 1.2 %copy.12 = f32[3,3,3,64,53]{3,4,2,1,0:T(8,128)} copy(f32[3,3,3,64,53]{4,3,2,1,0:T(8,128)S(1)} %bitcast.12) | data formatting | bytes 732672
  49.4 0.9 %copy.14 = f32[3,3,3,58,64]{4,3,2,1,0:T(8,128)} copy(f32[3,3,3,58,64]{4,3,2,1,0:T(8,128)S(1)} %bitcast.11) | data formatting | bytes 801792
  (2 shorter events, 0.0 us)
Async XLA Ops:
  1.7 0.9 %copy-start.2 = (bf16[4,4,58,128]{3,1,2,0:T(4,128)(2,1)S(1)}, bf16[4,4,58,128]{3,1,2,0:T(4,128)(2,1)}, u32[]{:S(2)}) copy-start(bf16[4,4,58,128]{3,1,2,0:T(4,128)(2,1)} %param.4) | copy-start | bytes 712708
  2.6 1.0 %copy-start = (bf16[3,3,3,58,64]{4,3,2,1,0:T(8,128)(2,1)S(1)}, bf16[3,3,3,58,64]{4,3,2,1,0:T(8,128)(2,1)}, u32[]{:S(2)}) copy-start(bf16[3,3,3,58,64]{4,3,2,1,0:T(8,128)(2,1)} %param.6) | copy-start | bytes 601348
  3.6 1.0 %copy-start.1 = (bf16[3,3,3,64,53]{3,4,2,1,0:T(8,128)(2,1)S(1)}, bf16[3,3,3,64,53]{3,4,2,1,0:T(8,128)(2,1)}, u32[]{:S(2)}) copy-start(bf16[3,3,3,64,53]{3,4,2,1,0:T(8,128)(2,1)} %param.7) | copy-start | bytes 549508

commit v3 on v2

--- a/solution.py
+++ b/solution.py
@@ -18,10 +18,10 @@
 
 def kernel(
     nx, ny, bx, by, depth, rows, normalizer,
-    x_ref, t_ref, w1_ref, w2_ref,
+    x_ref, t_ref, w1_hbm, w2_hbm,
     pred_ref, g1_ref, g2_ref,
     raw_in, raw_hid, raw_grad, sh_in, sh_hid, sh_grad, wide_grad, wide_slope,
-    first_w, second_w, back_w, act, acc, part, from_x, half, from_y, whole,
+    w1_ref, w2_ref, w_sem, first_w, second_w, back_w, act, acc, part, from_x, half, from_y, whole,
     halo_send, halo_recv, x_send, x_recv, y_send, y_recv, ay_send, ay_recv, ax_send, ax_recv,
 ):
     gx = lax.axis_index("gx")
@@ -30,6 +30,12 @@
     wide = lanes + 2 * depth
     inner = slice(depth, depth + lanes)
 
+    loads = [
+        pltpu.make_async_copy(w1_hbm, w1_ref, w_sem.at[0]),
+        pltpu.make_async_copy(w2_hbm, w2_ref, w_sem.at[1]),
+    ]
+    for load in loads:
+        load.start()
     for raw in (raw_in, raw_hid, raw_grad):
         raw[0] = jnp.zeros((CH, wide), bf16)
         raw[bx + 1] = jnp.zeros((CH, wide), bf16)
@@ -38,16 +44,45 @@
     raw_in[1 : bx + 1, :, inner] = x_ref[...]
 
     barrier = pltpu.get_barrier_semaphore()
-    for dx in range(nx):
-        for dy in range(ny):
-            if dx or dy:
-                pl.semaphore_signal(
-                    barrier,
-                    inc=1,
-                    device_id={"gx": lax.rem(gx + dx, nx), "gy": lax.rem(gy + dy, ny)},
-                    device_id_type=pl.DeviceIdType.MESH,
-                )
-    pl.semaphore_wait(barrier, nx * ny - 1)
+    def filled(block):
+        missing = CH - block.shape[0]
+        return jnp.concatenate([block.astype(f32), jnp.zeros((missing, CH), f32)], axis=0)
+
+    def turned(blocks):
+        stacked = jnp.concatenate([filled(block) for block in blocks], axis=0)
+        return stacked.T.astype(bf16)
+
+    def prepare():
+        for load in loads:
+            load.wait()
+        for b in range(3):
+            first_w[b * CH : (b + 1) * CH, :] = turned(
+                [w1_ref[(a * 3 + b) * 3 + c] for a in range(3) for c in range(3)]
+            )
+            for a in range(3):
+                for c in range(3):
+                    column = (a * 3 + c) * CH
+                    second_w[b * CH : (b + 1) * CH, column : column + CH] = filled(
+                        w2_ref[(a * 3 + b) * 3 + c]
+                    ).astype(bf16)
+
+    def greet(x, y):
+        pl.semaphore_signal(
+            barrier, inc=1, device_id={"gx": x, "gy": y}, device_id_type=pl.DeviceIdType.MESH
+        )
+
+    for dx, dy in DIRECTIONS[4:]:
+        x, y = gx + dx, gy + dy
+        pl.when((x >= 0) & (x < nx) & (y >= 0) & (y < ny))(
+            functools.partial(greet, lax.rem(x + nx, nx), lax.rem(y + ny, ny))
+        )
+    for d in range(1, nx):
+        greet(lax.rem(gx + d, nx), gy)
+    for d in range(1, ny):
+        greet(gx, lax.rem(gy + d, ny))
+    beside_x = lax.div(gx + nx - 1, nx) + lax.div(2 * nx - 2 - gx, nx)
+    beside_y = lax.div(gy + ny - 1, ny) + lax.div(2 * ny - 2 - gy, ny)
+    pl.semaphore_wait(barrier, nx + ny - 2 + beside_x * beside_y)
 
     def spans(step, count, unit):
         source = {0: (1, count), 1: (count, 1), -1: (1, 1)}[step]
@@ -156,8 +191,8 @@
     def span_y(index):
         return pl.ds(pl.multiple_of(index * rows, 16), rows)
 
-    def span_own():
-        return pl.ds(pl.multiple_of((gx * ny + gy) * rows, 16), rows)
+    def span_own(y):
+        return pl.ds(pl.multiple_of((gx * ny + y) * rows, 16), rows)
 
     def scatter_x(slot):
         copies = []
@@ -191,12 +226,12 @@
         for d, copy in enumerate(copies):
             copy.wait_recv()
             total = total + from_y[slot, d].astype(f32)
-        whole[slot, span_own()] = total.astype(bf16)
+        whole[slot, span_own(gy)] = total.astype(bf16)
         result = []
         for d in range(1, ny):
             to = lax.rem(gy + d, ny)
             result.append(remote(
-                whole.at[slot, span_own()], whole.at[slot, span_own()],
+                whole.at[slot, span_own(gy)], whole.at[slot, span_own(gy)],
                 ay_send.at[slot, d - 1], ay_recv.at[slot, d - 1], {"gy": to},
             ))
             result[-1].start()
@@ -229,20 +264,9 @@
             out[a, 1] = both[a * third : (a + 1) * third, CH:]
             out[a, 2] = rest[a * third : (a + 1) * third]
 
-    def turned(blocks):
-        stacked = jnp.concatenate([block.astype(f32) for block in blocks], axis=0)
-        return stacked.T.astype(bf16)
-
     in_copies = halo(raw_in, 0)
     start(in_copies)
-    for b in range(3):
-        first_w[b * CH : (b + 1) * CH, :] = turned(
-            [w1_ref[(a * 3 + b) * 3 + c] for a in range(3) for c in range(3)]
-        )
-        for a in range(3):
-            for c in range(3):
-                column = (a * 3 + c) * CH
-                second_w[b * CH : (b + 1) * CH, column : column + CH] = w2_ref[(a * 3 + b) * 3 + c]
+    prepare()
     arrive(in_copies)
     shift(raw_in, sh_in)
 
@@ -329,8 +353,7 @@
         return jnp.pad(rolled, ((0, 0), (0, CH - field.shape[2]), (0, 0)))
 
     def taps(w):
-        w = jnp.pad(w, ((0, 0),) * 3 + ((0, CH - w.shape[3]), (0, CH - w.shape[4])))
-        return w.reshape(27, CH, CH)
+        return w.reshape((27,) + w.shape[3:])
 
     lanes = by * depth
     wide = lanes + 2 * depth
@@ -345,12 +368,13 @@
             jax.ShapeDtypeStruct((3, 3, 3 * CH, CH), f32),
             jax.ShapeDtypeStruct((3, 3, 3 * CH, CH), f32),
         ),
-        in_specs=[vmem] * 4,
+        in_specs=[vmem] * 2 + [pl.BlockSpec(memory_space=pl.ANY)] * 2,
         out_specs=(vmem,) * 3,
         scratch_shapes=(
             [pltpu.VMEM((bx + 2, CH, wide), bf16)] * 3
             + [pltpu.VMEM((bx + 2, 3 * CH, wide), bf16)] * 3
             + [pltpu.VMEM((bx, 3 * CH, wide), bf16)] * 2
+            + [pltpu.VMEM((27, cin, hid), bf16), pltpu.VMEM((27, cout, hid), bf16), dma((2,))]
             + [pltpu.VMEM((3 * CH, 9 * CH), bf16)] * 3
             + [
                 pltpu.VMEM((bx, CH, lanes), f32),

time: 50.6 us -> 50 us (0.988)
  local copies, waits for them, and re-layouts: 7.01 us -> 6.04 us
    unnamed x8, local copies, waits for them, and re-layouts: 4.8 us -> 4.06 us
where the time goes in v3:
time: 50 us; the launch traced here: 49.8 us
  Pallas kernels  43.1 us (86%)
  local copies, waits for them, and re-layouts  6.04 us (12%)
  between operations  0.68 us (1%)
    pallas_call x1, Pallas kernels, on_device(): pl.pallas_call(functools.partial(kernel, nx, ny, bx, by, depth, rows, nor...  43.1 us
    unnamed x8, local copies, waits for them, and re-layouts  4.06 us
    reshape x2, local copies, waits for them, and re-layouts, flat(): rolled = field.transpose(0, 2, 1, 3).reshape(bx, field.shape[2], by * depth)  1.12 us

profile of v3, /device:TPU:1, one launch (start us, length us, event | category | flops | bytes accessed | tf_op | source)
XLA Modules:
  0.0 49.8 jit_solution(9535586294198174101)
XLA Ops:
  0.6 1.0 %reshape.28 = bf16[4,53,512]{2,1,0:T(8,128)(2,1)S(1)} reshape(bf16[4,53,4,128]{3,2,1,0:T(4,128)(2,1)} %bitcast.17) | data formatting | bytes 434176 | tf_op jit(solution)/shard_map/reshape | solution.py:352
  1.7 0.0 copy-start.2
  1.7 0.9 %copy-done.2 = bf16[4,4,58,128]{3,1,2,0:T(4,128)(2,1)S(1)} copy-done((bf16[4,4,58,128]{3,1,2,0:T(4,128)(2,1)S(1)}, bf16[4,4,58,128]{3,1,2,0:T(4,128)(2,1)}, u32[]{:S(2)}) %copy-start.2) | copy-done | bytes 237592
  2.6 0.0 copy-start
  2.6 0.1 reshape.34
  2.7 0.0 copy-start.1
  2.7 0.9 %copy-done = bf16[3,3,3,58,64]{4,3,2,1,0:T(8,128)(2,1)S(1)} copy-done((bf16[3,3,3,58,64]{4,3,2,1,0:T(8,128)(2,1)S(1)}, bf16[3,3,3,58,64]{4,3,2,1,0:T(8,128)(2,1)}, u32[]{:S(2)}) %copy-start) | copy-done | bytes 200472
  3.6 0.1 copy-done.1
  3.8 43.1 %shard_map.67 = (bf16[4,64,512]{2,1,0:T(8,128)(2,1)S(1)}, f32[3,3,192,64]{3,2,1,0:T(8,128)S(1)}, f32[3,3,192,64]{3,2,1,0:T(8,128)S(1)}) custom-call(bf16[4,64,512]{2,1,0:T(8,128)(2,1)S(1)} %pad.8.x_ref, bf16[4,64,512]{2,1,0:T(8,128)(2,1)S(1)} %pad.9.t_ref, bf16[27,58,64]{2,1,0:T(8,128)(2,1)S(1)} %bitcast.14, bf16[27,53,64]{2,1,0:T(8,128)(2,1)S(1)} %bitcast.15), custom_call_target="tpu_custom_call" | custom-call | flops 3397386240 | bytes 8388608 | tf_op jit(solution)/shard_map/pallas_call | solution.py:364
  46.8 0.1 reshape.31
  46.9 0.8 %slice_bitcast_fusion = bf16[4,4,53,128]{3,1,2,0:T(4,128)(2,1)} fusion(bf16[4,64,4,128]{3,2,1,0:T(4,128)(2,1)S(1)} %reshape.31), kind=kLoop, calls=%fused_computation | loop fusion | bytes 434176 | tf_op jit(solution)/shard_map/transpose | solution.py:406
  47.6 1.2 %copy.12 = f32[3,3,3,64,53]{3,4,2,1,0:T(8,128)} copy(f32[3,3,3,64,53]{4,3,2,1,0:T(8,128)S(1)} %bitcast.13) | data formatting | bytes 732672
  48.9 0.9 %copy.14 = f32[3,3,3,58,64]{4,3,2,1,0:T(8,128)} copy(f32[3,3,3,58,64]{4,3,2,1,0:T(8,128)S(1)} %bitcast.12) | data formatting | bytes 801792
  (2 shorter events, 0.0 us)
Async XLA Ops:
  1.7 0.9 %copy-start.2 = (bf16[4,4,58,128]{3,1,2,0:T(4,128)(2,1)S(1)}, bf16[4,4,58,128]{3,1,2,0:T(4,128)(2,1)}, u32[]{:S(2)}) copy-start(bf16[4,4,58,128]{3,1,2,0:T(4,128)(2,1)} %param.4) | copy-start | bytes 712708
  2.6 1.0 %copy-start = (bf16[3,3,3,58,64]{4,3,2,1,0:T(8,128)(2,1)S(1)}, bf16[3,3,3,58,64]{4,3,2,1,0:T(8,128)(2,1)}, u32[]{:S(2)}) copy-start(bf16[3,3,3,58,64]{4,3,2,1,0:T(8,128)(2,1)} %param.6) | copy-start | bytes 601348
  2.7 1.1 %copy-start.1 = (bf16[3,3,3,64,53]{3,4,2,1,0:T(8,128)(2,1)S(1)}, bf16[3,3,3,64,53]{3,4,2,1,0:T(8,128)(2,1)}, u32[]{:S(2)}) copy-start(bf16[3,3,3,64,53]{3,4,2,1,0:T(8,128)(2,1)} %param.7) | copy-start | bytes 549508

commit v4 on v3

--- a/solution.py
+++ b/solution.py
@@ -168,7 +168,7 @@
             )
             return 0
 
-        lax.fori_loop(0, bx, body, 0)
+        lax.fori_loop(0, bx, body, 0, unroll=True)
         used = 9 * CH
         mid = used // 2
         part[slot, :used, :] = acc[:, : 2 * CH].astype(bf16)
@@ -277,7 +277,7 @@
         raw_hid[x + 1, :, inner] = (0.5 * value * (1.0 + tangent)).astype(bf16)
         return 0
 
-    lax.fori_loop(0, bx, first_layer, 0)
+    lax.fori_loop(0, bx, first_layer, 0, unroll=True)
     hid_copies = halo(raw_hid, 1)
     start(hid_copies)
     for b in range(3):
@@ -293,7 +293,7 @@
         ) * root_two_pi * (1.0 + 3.0 * cubic_term * value * value)
         return 0
 
-    lax.fori_loop(0, bx, slopes, 0)
+    lax.fori_loop(0, bx, slopes, 0, unroll=True)
     arrive(hid_copies)
     shift(raw_hid, sh_hid)
 
@@ -305,7 +305,7 @@
         spread(wide_grad, x, grad)
         return 0
 
-    lax.fori_loop(0, bx, second_layer, 0)
+    lax.fori_loop(0, bx, second_layer, 0, unroll=True)
     grad_copies = halo(raw_grad, 2)
     start(grad_copies)
     filter_grad(sh_hid, wide_grad, 1)
@@ -318,7 +318,7 @@
         spread(wide_slope, x, (value * act[x]).astype(bf16))
         return 0
 
-    lax.fori_loop(0, bx, back, 0)
+    lax.fori_loop(0, bx, back, 0, unroll=True)
     scatter_y_second = scatter_y(1, scatter_x_second)
     filter_grad(sh_in, wide_slope, 0)
     scatter_x_first = scatter_x(0)

time: 50 us -> 47.7 us (0.954)
  Pallas kernels: 43.1 us -> 40.8 us
    pallas_call x1, Pallas kernels: 43.1 us -> 40.8 us  [on_device(): pl.pallas_call(functools.partial(kernel, nx, ny, bx, by, depth, rows, nor...]
where the time goes in v4:
time: 47.7 us; the launch traced here: 47.5 us
  Pallas kernels  40.8 us (86%)
  local copies, waits for them, and re-layouts  6.04 us (13%)
  between operations  0.68 us (1%)
    pallas_call x1, Pallas kernels, on_device(): pl.pallas_call(functools.partial(kernel, nx, ny, bx, by, depth, rows, nor...  40.8 us
    unnamed x8, local copies, waits for them, and re-layouts  4.06 us
    reshape x2, local copies, waits for them, and re-layouts, flat(): rolled = field.transpose(0, 2, 1, 3).reshape(bx, field.shape[2], by * depth)  1.12 us

profile of v4, /device:TPU:1, one launch (start us, length us, event | category | flops | bytes accessed | tf_op | source)
XLA Modules:
  0.0 47.5 jit_solution(17937221903664368191)
XLA Ops:
  0.6 1.0 %reshape.28 = bf16[4,53,512]{2,1,0:T(8,128)(2,1)S(1)} reshape(bf16[4,53,4,128]{3,2,1,0:T(4,128)(2,1)} %bitcast.17) | data formatting | bytes 434176 | tf_op jit(solution)/shard_map/reshape | solution.py:352
  1.7 0.0 copy-start.2
  1.7 0.9 %copy-done.2 = bf16[4,4,58,128]{3,1,2,0:T(4,128)(2,1)S(1)} copy-done((bf16[4,4,58,128]{3,1,2,0:T(4,128)(2,1)S(1)}, bf16[4,4,58,128]{3,1,2,0:T(4,128)(2,1)}, u32[]{:S(2)}) %copy-start.2) | copy-done | bytes 237592
  2.6 0.0 copy-start
  2.6 0.1 reshape.34
  2.7 0.0 copy-start.1
  2.7 0.9 %copy-done = bf16[3,3,3,58,64]{4,3,2,1,0:T(8,128)(2,1)S(1)} copy-done((bf16[3,3,3,58,64]{4,3,2,1,0:T(8,128)(2,1)S(1)}, bf16[3,3,3,58,64]{4,3,2,1,0:T(8,128)(2,1)}, u32[]{:S(2)}) %copy-start) | copy-done | bytes 200472
  3.6 0.1 copy-done.1
  3.8 40.8 %shard_map.67 = (bf16[4,64,512]{2,1,0:T(8,128)(2,1)S(1)}, f32[3,3,192,64]{3,2,1,0:T(8,128)S(1)}, f32[3,3,192,64]{3,2,1,0:T(8,128)S(1)}) custom-call(bf16[4,64,512]{2,1,0:T(8,128)(2,1)S(1)} %pad.8.x_ref, bf16[4,64,512]{2,1,0:T(8,128)(2,1)S(1)} %pad.9.t_ref, bf16[27,58,64]{2,1,0:T(8,128)(2,1)S(1)} %bitcast.14, bf16[27,53,64]{2,1,0:T(8,128)(2,1)S(1)} %bitcast.15), custom_call_target="tpu_custom_call" | custom-call | flops 3397386240 | bytes 8388608 | tf_op jit(solution)/shard_map/pallas_call | solution.py:364
  44.6 0.1 reshape.31
  44.6 0.8 %slice_bitcast_fusion = bf16[4,4,53,128]{3,1,2,0:T(4,128)(2,1)} fusion(bf16[4,64,4,128]{3,2,1,0:T(4,128)(2,1)S(1)} %reshape.31), kind=kLoop, calls=%fused_computation | loop fusion | bytes 434176 | tf_op jit(solution)/shard_map/transpose | solution.py:406
  45.4 1.2 %copy.12 = f32[3,3,3,64,53]{3,4,2,1,0:T(8,128)} copy(f32[3,3,3,64,53]{4,3,2,1,0:T(8,128)S(1)} %bitcast.13) | data formatting | bytes 732672
  46.6 0.9 %copy.14 = f32[3,3,3,58,64]{4,3,2,1,0:T(8,128)} copy(f32[3,3,3,58,64]{4,3,2,1,0:T(8,128)S(1)} %bitcast.12) | data formatting | bytes 801792
  (2 shorter events, 0.0 us)
Async XLA Ops:
  1.7 0.9 %copy-start.2 = (bf16[4,4,58,128]{3,1,2,0:T(4,128)(2,1)S(1)}, bf16[4,4,58,128]{3,1,2,0:T(4,128)(2,1)}, u32[]{:S(2)}) copy-start(bf16[4,4,58,128]{3,1,2,0:T(4,128)(2,1)} %param.4) | copy-start | bytes 712708
  2.6 1.0 %copy-start = (bf16[3,3,3,58,64]{4,3,2,1,0:T(8,128)(2,1)S(1)}, bf16[3,3,3,58,64]{4,3,2,1,0:T(8,128)(2,1)}, u32[]{:S(2)}) copy-start(bf16[3,3,3,58,64]{4,3,2,1,0:T(8,128)(2,1)} %param.6) | copy-start | bytes 601348
  2.7 1.1 %copy-start.1 = (bf16[3,3,3,64,53]{3,4,2,1,0:T(8,128)(2,1)S(1)}, bf16[3,3,3,64,53]{3,4,2,1,0:T(8,128)(2,1)}, u32[]{:S(2)}) copy-start(bf16[3,3,3,64,53]{3,4,2,1,0:T(8,128)(2,1)} %param.7) | copy-start | bytes 549508
